TPU v7x, 256 devices: a whole 4x4x8 slice. The times are simulated.
256 devices in a mesh: tm: 8 (over z), atom: 2 (over x_lo), chan: 16 (over y, x_hi, core).
Axes of the slice: x: 4 (x_hi: 2, x_lo: 2; x = x_hi * 2 + x_lo), y: 4, z: 8, core: 2. Of those that a mesh axis runs over, the one named last changes fastest.
Arguments:
- signal: bfloat16 [256, 8192], P('chan', 'tm'), may hold values from -6 to 6
- codes_init: float32 [128, 8192], P('atom', 'tm'), may hold values from -4 to 4
- atom_bank: bfloat16 [128, 256, 512], P('atom', 'chan'), may hold values from -0.015625 to 0.015625
- step_size: float32 [128], P('atom'), may hold values from 0.1 to 0.5
- threshold: float32 [128], P('atom'), may hold values from 0.3 to 3
Outputs:
- final_codes: float32 [128, 8192], P('atom', 'tm')
- residual: float32 [256, 8192], P('chan', 'tm')
All inputs are finite; a program needn't handle non-finite values.
Results may differ from a plain program's by a relative error of at most 0.0025.
Values may be sent and summed in bfloat16 or wider, within the bound.
A program may use at most 64 MiB of HBM per device.

v0:
```python
import jax
import jax.numpy as jnp
from jax import lax
from jax.sharding import PartitionSpec as P

ITERS = 2


def from_behind(value, axis, steps):
    count = lax.axis_size(axis)
    leading, last = (max(0, -steps), min(count, count - steps))
    return lax.ppermute(value, axis, [(source, source + steps) for source in range(leading, last)])


def synthesize(extended, atom_bank):
    atom_rows, chan_rows, taps = atom_bank.shape
    group = min(32, taps)
    turns = taps // group
    length = extended.shape[1] - taps + 1
    weights = (
        atom_bank.reshape(atom_rows, chan_rows, turns, group)
        .transpose(2, 1, 3, 0)
        .reshape(turns, chan_rows, group * atom_rows)
    )

    def synthesize_accumulate(turn_index, total):
        start = taps - group - turn_index * group
        window = lax.dynamic_slice_in_dim(extended, start, length + group - 1, 1)
        stacked = jnp.concatenate(
            [
                window[:, group - 1 - offset : group - 1 - offset + length]
                for offset in range(group)
            ],
            axis=0,
        )
        return total + jnp.dot(weights[turn_index], stacked, preferred_element_type=jnp.float32)

    return lax.fori_loop(
        0, turns, synthesize_accumulate, jnp.zeros((chan_rows, length), jnp.float32)
    )


def correlate(extended, atom_bank):
    atom_rows, chan_rows, taps = atom_bank.shape
    group = min(32, taps)
    turns = taps // group
    length = extended.shape[1] - taps + 1
    weights = (
        atom_bank.reshape(atom_rows, chan_rows, turns, group)
        .transpose(2, 0, 3, 1)
        .reshape(turns, atom_rows, group * chan_rows)
    )

    def correlate_accumulate(turn_index, total):
        start = turn_index * group
        window = lax.dynamic_slice_in_dim(extended, start, length + group - 1, 1)
        stacked = jnp.concatenate(
            [window[:, offset : offset + length] for offset in range(group)], axis=0
        )
        return total + jnp.dot(weights[turn_index], stacked, preferred_element_type=jnp.float32)

    return lax.fori_loop(
        0, turns, correlate_accumulate, jnp.zeros((atom_rows, length), jnp.float32)
    )


def shrink(current, gradient, step_size, threshold):
    moved = current - step_size[:, None] * gradient
    bound = (step_size * threshold)[:, None]
    return moved - jnp.clip(moved, -bound, bound)


def body(signal, codes_init, atom_bank, step_size, threshold):
    taps = atom_bank.shape[2]
    slab = signal.shape[1]
    current = codes_init
    misfit = None
    for sweep_index in range(ITERS):
        lowered = current.astype(jnp.bfloat16)
        earlier = from_behind(lowered[:, slab - taps + 1 :], "tm", 1)
        partial_recon = synthesize(jnp.concatenate([earlier, lowered], axis=1), atom_bank)
        recon = lax.psum(partial_recon, "atom")
        misfit = recon - signal.astype(jnp.float32)
        rounded = misfit.astype(jnp.bfloat16)
        following = from_behind(rounded[:, : taps - 1], "tm", -1)
        partial_grad = correlate(jnp.concatenate([rounded, following], axis=1), atom_bank)
        gradient = lax.psum(partial_grad, "chan")
        current = shrink(current, gradient, step_size, threshold)
    return (current, misfit)


def solution(mesh):
    placed = (P("chan", "tm"), P("atom", "tm"), P("atom", "chan", None), P("atom"), P("atom"))
    return jax.shard_map(
        body,
        mesh=mesh,
        in_specs=placed,
        out_specs=(P("atom", "tm"), P("chan", "tm")),
        check_vma=False,
    )
```

profile of v0, /device:TPU:1, one launch (start us, length us, event | category | flops | bytes accessed | tf_op | source)
XLA Modules:
  0.0 1402.1 jit_solution(5570843952976790271)
XLA Ops:
  8.3 4.4 collective-permute-start
  12.7 2.4 copy.9
  15.0 1.6 reshape.24
  16.7 1.6 copy.11
  18.4 435.2 %while.60 = (s32[]{:T(128)}, f32[16,1024]{1,0:T(8,128)S(1)}, bf16[16,16,2048]{2,1,0:T(8,128)(2,1)}, bf16[64,1535]{1,0:T(8,128)(2,1)S(1)}, s32[]{:T(128)}, /*inde...) while((s32[]{:T(128)}, f32[16,1024]{1,0:T(8,128)S(1)}, ...), condition=%wide.region_1.0_spmd.clone, body=%wide.region_0.0_spmd.clone.sunk | while | flops 67141672 | bytes 12780941 | solution.py:38
  42.7 2.9 convolution_add_fusion.8
  69.9 2.9 convolution_add_fusion.8
  97.1 2.9 convolution_add_fusion.8
  124.3 2.9 convolution_add_fusion.8
  151.5 2.9 convolution_add_fusion.8
  178.7 2.9 convolution_add_fusion.8
  205.9 2.9 convolution_add_fusion.8
  233.1 2.9 convolution_add_fusion.8
  260.3 2.9 convolution_add_fusion.8
  287.5 2.9 convolution_add_fusion.8
  314.7 2.9 convolution_add_fusion.8
  341.9 2.9 convolution_add_fusion.8
  369.1 2.9 convolution_add_fusion.8
  396.3 2.9 convolution_add_fusion.8
  423.5 2.9 convolution_add_fusion.8
  450.7 2.9 convolution_add_fusion.8
  454.3 34.5 %all-reduce.5.cloned.1.call-done = f32[16,1024]{1,0:T(8,128)} async-done(((f32[16,1024]{1,0:T(8,128)}), f32[16,1024]{1,0:T(8,128)}) %all-reduce.5.cloned.1.call-update) | async-done | bytes 65552 | tf_op jit(solution)/shard_map/psum | solution.py:82
  489.7 1.3 collective-permute-start.1
  491.0 2.7 copy.15
  493.7 1.6 copy.12
  495.4 61.8 %while.61 = (s32[]{:T(128)}, f32[64,1024]{1,0:T(8,128)S(1)}, bf16[16,64,512]{2,1,0:T(8,128)(2,1)}, bf16[16,1535]{1,0:T(8,128)(2,1)S(1)}, s32[]{:T(128)}, /*index...) while((s32[]{:T(128)}, f32[64,1024]{1,0:T(8,128)S(1)}, ...), condition=%wide.region_4.0_spmd.clone, body=%wide.region_3.0_spmd.clone.sunk | while | flops 67239976 | bytes 3736953 | solution.py:62
  498.1 1.2 convolution_add_fusion.9
  501.9 1.2 convolution_add_fusion.9
  505.8 1.2 convolution_add_fusion.9
  509.7 1.2 convolution_add_fusion.9
  513.5 1.2 convolution_add_fusion.9
  517.4 1.2 convolution_add_fusion.9
  521.3 1.2 convolution_add_fusion.9
  525.1 1.2 convolution_add_fusion.9
  529.0 1.2 convolution_add_fusion.9
  536.7 1.2 convolution_add_fusion.9
  558.0 145.2 %all-reduce.7.cloned.1.call-done = f32[64,1024]{1,0:T(8,128)} async-done(((f32[64,1024]{1,0:T(8,128)}), f32[64,1024]{1,0:T(8,128)}) %all-reduce.7.cloned.1.call-update) | async-done | bytes 262160 | tf_op jit(solution)/shard_map/psum | solution.py:87
  704.4 3.4 collective-permute-start.2
  709.0 435.2 %while.62 = (s32[]{:T(128)}, f32[16,1024]{1,0:T(8,128)S(1)}, bf16[16,16,2048]{2,1,0:T(8,128)(2,1)}, bf16[64,1535]{1,0:T(8,128)(2,1)S(1)}, s32[]{:T(128)}, /*inde...) while((s32[]{:T(128)}, f32[16,1024]{1,0:T(8,128)S(1)}, ...), condition=%wide.region_7.8_spmd.clone, body=%wide.region_6.7_spmd.clone.sunk | while | flops 67141672 | bytes 12780941 | solution.py:38
  733.4 2.9 convolution_add_fusion.10
  760.6 2.9 convolution_add_fusion.10
  787.8 2.9 convolution_add_fusion.10
  815.0 2.9 convolution_add_fusion.10
  842.2 2.9 convolution_add_fusion.10
  869.4 2.9 convolution_add_fusion.10
  896.6 2.9 convolution_add_fusion.10
  923.8 2.9 convolution_add_fusion.10
  951.0 2.9 convolution_add_fusion.10
  978.2 2.9 convolution_add_fusion.10
  1005.4 2.9 convolution_add_fusion.10
  1032.6 2.9 convolution_add_fusion.10
  1059.8 2.9 convolution_add_fusion.10
  1087.0 2.9 convolution_add_fusion.10
  1114.2 2.9 convolution_add_fusion.10
  1141.4 2.9 convolution_add_fusion.10
  1145.0 35.0 %all-reduce.9.cloned.1.call-done = f32[16,1024]{1,0:T(8,128)} async-done(((f32[16,1024]{1,0:T(8,128)}), f32[16,1024]{1,0:T(8,128)}) %all-reduce.9.cloned.1.call-update) | async-done | bytes 65552 | tf_op jit(solution)/shard_map/psum | solution.py:82
  1180.0 1.5 fusion.14
  1181.5 1.3 collective-permute-start.3
  1182.8 3.2 collective-permute-done.3
  1186.0 61.8 %while.63 = (s32[]{:T(128)}, f32[64,1024]{1,0:T(8,128)S(1)}, bf16[16,64,512]{2,1,0:T(8,128)(2,1)}, bf16[16,1535]{1,0:T(8,128)(2,1)S(1)}, s32[]{:T(128)}, /*index...) while((s32[]{:T(128)}, f32[64,1024]{1,0:T(8,128)S(1)}, ...), condition=%wide.region_10.11_spmd.clone, body=%wide.region_9.10_spmd.clone.sunk | while | flops 67239976 | bytes 3736953 | solution.py:62
  1219.6 1.2 convolution_add_fusion.11
  1246.6 1.2 convolution_add_fusion.11
  1248.5 145.2 %all-reduce.11.cloned.1.call-done = f32[64,1024]{1,0:T(8,128)} async-done(((f32[64,1024]{1,0:T(8,128)}), f32[64,1024]{1,0:T(8,128)}) %all-reduce.11.cloned.1.call-update) | async-done | bytes 262160 | tf_op jit(solution)/shard_map/psum | solution.py:87
  1393.7 1.8 minimum_subtract_fusion
  (2115 shorter events, 893.4 us)
Async XLA Ops:
  7.2 481.7 %all-reduce.5.cloned.1.call-start = ((), (), s32[]{:S(2)}) async-start(), calls=%async_computation | async-start | bytes 131072 | tf_op jit(solution)/shard_map/psum | solution.py:82
  8.3 10.0 collective-permute-start
  18.4 470.5 %copy-start.7 = (bf16[16,1024]{1,0:T(8,128)(2,1)S(1)}, bf16[16,1024]{1,0:T(8,128)(2,1)}, u32[]{:S(2)}) copy-start(bf16[16,1024]{1,0:T(8,128)(2,1)} %param.13) | copy-start | bytes 98308
  18.4 472.6 %copy-start.2 = (bf16[64,16,512]{2,1,0:T(8,128)(2,1)S(1)}, bf16[64,16,512]{2,1,0:T(8,128)(2,1)}, u32[]{:S(2)}) copy-start(bf16[64,16,512]{2,1,0:T(8,128)(2,1)} %param.15) | copy-start | bytes 3145732
  453.6 0.6 copy-start.3
  454.3 249.0 %all-reduce.7.cloned.1.call-start = ((), (), s32[]{:S(2)}) async-start(), calls=%async_computation.1 | async-start | bytes 524288 | tf_op jit(solution)/shard_map/psum | solution.py:87
  489.7 5.6 collective-permute-start.1
  495.3 62.7 %copy-start.8 = (f32[64]{0:T(128)S(1)}, f32[64]{0:T(128)}, u32[]{:S(2)}) copy-start(f32[64]{0:T(128)} %param.16) | copy-start | bytes 772
  495.3 62.7 %copy-start.9 = (f32[64]{0:T(128)S(1)}, f32[64]{0:T(128)}, u32[]{:S(2)}) copy-start(f32[64]{0:T(128)} %param.17) | copy-start | bytes 772
  495.3 207.9 %copy-start.5 = (f32[64,1024]{1,0:T(8,128)S(1)}, f32[64,1024]{1,0:T(8,128)}, u32[]{:S(2)}) copy-start(f32[64,1024]{1,0:T(8,128)} %param.14) | copy-start | bytes 786436
  557.2 0.7 copy-start
  557.9 622.0 %all-reduce.9.cloned.1.call-start = ((), (), s32[]{:S(2)}) async-start(), calls=%async_computation.2 | async-start | bytes 131072 | tf_op jit(solution)/shard_map/psum | solution.py:82
  704.4 4.5 collective-permute-start.2
  1144.2 0.6 copy-start.4
  1144.9 248.8 %all-reduce.11.cloned.1.call-start = ((), (), s32[]{:S(2)}) async-start(), calls=%async_computation.3 | async-start | bytes 524288 | tf_op jit(solution)/shard_map/psum | solution.py:87
  1181.5 4.5 collective-permute-start.3
  1185.9 207.8 %copy-start.6 = (f32[64,1024]{1,0:T(8,128)S(1)}, f32[64,1024]{1,0:T(8,128)}, u32[]{:S(2)}) copy-start(f32[64,1024]{1,0:T(8,128)} %all-reduce.7.cloned.1.call-done) | copy-start | bytes 786436
  1247.8 0.7 copy-start.1
Sparse Core Ops, SparseCore 0:
  454.4 34.3 all-reduce.4
  558.1 145.1 all-reduce.6
  1145.0 34.9 all-reduce.8
  1248.7 145.0 all-reduce.10
where the time goes:
time: 1400 us
  local copies, waits for them, and re-layouts  876 us (63%)
  waiting for transfers between devices  364 us (26%)
  matrix products  129 us (9%)
  between operations  14 us (1%)
    while x1984, local copies, waits for them, and re-layouts  836 us
    psum x2, waiting for transfers between devices, body(): gradient = lax.psum(partial_grad, 'chan')  290 us
    dot_general x32, matrix products, synthesize_accumulate(): jnp.dot(weights[turn_index], stacked, preferred_element_type=jnp.float32)  92.1 us
    psum x2, waiting for transfers between devices, body(): recon = lax.psum(partial_recon, 'atom')  69.5 us
    dot_general x32, matrix products, correlate_accumulate(): jnp.dot(weights[turn_index], stacked, preferred_element_type=jnp.float32)  37 us
  transfers between devices with their start and end apart: 8, of which 6 were waited for; matrix products, arithmetic and copies ran while one was open for 1% of the time, Pallas kernels for 0%

commit v1 on v0

v1 whole, which is shorter than its diff:
```python
import functools

import jax
import jax.numpy as jnp
from jax import lax
from jax.experimental import pallas as pl
from jax.experimental.pallas import tpu as pltpu
from jax.sharding import PartitionSpec as P

F32, BF16 = jnp.float32, jnp.bfloat16
MESH = pl.DeviceIdType.MESH
ITERS = 2
ATOMS, CHANS, TAPS, SLAB = 64, 16, 512, 1024
LANES, HALF = 128, 512
GROUP = 16


def tile_iota(rows, columns, dimension):
    return lax.broadcasted_iota(jnp.int32, (rows, columns), dimension)


def matmul(left, right):
    return jnp.dot(left, right, preferred_element_type=F32)


def arrange_bank(bank, natural, synthesis, gradient):
    row, column = tile_iota(256, 256, 0), tile_iota(256, 256, 1)
    swap = ((row // 16 == column % 16) & (row % 16 == column // 16)).astype(BF16)
    for part in range(4):
        swapped = matmul(swap, bank[256 * part : 256 * part + 256, :]).astype(BF16)
        for c in range(CHANS):
            for h in range(4):
                natural[64 * h + 16 * part : 64 * h + 16 * part + 16, 128 * c : 128 * c + 128] = (
                    swapped[16 * c : 16 * c + 16, 128 * h : 128 * h + 128]
                )
    eye = (tile_iota(128, 128, 0) == tile_iota(128, 128, 1)).astype(BF16)
    for c in range(CHANS):
        turned = lax.dot_general(
            eye,
            natural[:, 128 * c : 128 * c + 128],
            (((1,), (1,)), ((), ())),
            preferred_element_type=F32,
        ).astype(BF16)
        for j in range(8):
            synthesis[16 * c : 16 * c + 16, 256 * j : 256 * j + 256] = turned[16 * j : 16 * j + 16, :]
    row, column = tile_iota(512, 512, 0), tile_iota(512, 512, 1)
    select = (
        (row // 128 == column // 32 % 4)
        & (row // 32 % 4 == column // 128)
        & (row % 32 == 31 - column % 32)
    ).astype(BF16)
    for cg in range(4):
        moved = matmul(natural[:, 512 * cg : 512 * cg + 512], select).astype(BF16)
        for h in range(4):
            for q in range(4):
                at = 128 * (4 * cg + h)
                gradient[64 * q : 64 * q + 64, at : at + 128] = moved[
                    64 * h : 64 * h + 64, 128 * q : 128 * q + 128
                ]


def shift_codes(codes, keep, shifted, place):
    width = codes.shape[1]
    for j in range(8):
        shifted[j, :, place : place + keep] = pltpu.roll(codes, width - (113 - 16 * j), 1)[:, :keep]


def synthesize(shifted, synthesis, spread, begin, end):
    for start in range(begin, end, 256):
        stop = min(start + 256, end)
        total = None
        for j in range(8):
            window = jnp.concatenate(
                [shifted[j, :, start - 128 * h + 384 : stop - 128 * h + 384] for h in range(4)], axis=0
            )
            part = matmul(synthesis[:, 256 * j : 256 * j + 256], window)
            total = part if total is None else total + part
        spread[:, start:stop] = total


def gather_rows(spread, begin):
    rows = []
    for c in range(CHANS):
        low = spread[16 * c : 16 * c + 8, begin : begin + 640]
        high = spread[16 * c + 8 : 16 * c + 16, begin : begin + 640]
        both = pltpu.roll(low, 640 - 15, 1, stride=1, stride_axis=0) + pltpu.roll(
            high, 640 - 7, 1, stride=1, stride_axis=0
        )
        rows.append(jnp.sum(both[:, :HALF], axis=0, keepdims=True))
    return jnp.concatenate(rows, axis=0)


def shift_misfit(misfit, first, last, drop, shifted):
    begin, end = 128 * (first + drop), 128 * last
    for c in range(CHANS):
        row = jnp.broadcast_to(misfit[c : c + 1, 128 * first : end], (16, end - 128 * first)).astype(BF16)
        near = pltpu.roll(row, 1, 1, stride=1, stride_axis=0)
        far = pltpu.roll(near, 16, 1)
        at = 32 * (c % 4)
        shifted[c // 4, at : at + 16, begin:end] = near[:, 128 * drop :]
        shifted[c // 4, at + 16 : at + 32, begin:end] = far[:, 128 * drop :]


def correlate(shifted, gradient, spread, begin, end):
    for start in range(begin, end, 256):
        stop = min(start + 256, end)
        total = None
        for cg in range(4):
            for h in (0, 2):
                window = jnp.concatenate(
                    [
                        shifted[cg, :, start + 128 * h : stop + 128 * h],
                        shifted[cg, :, start + 128 * h + 128 : stop + 128 * h + 128],
                    ],
                    axis=0,
                )
                at = 128 * (4 * cg + h)
                part = matmul(gradient[:, at : at + 256], window)
                total = part if total is None else total + part
        spread[:, start:stop] = total


def gather_taps(spread, begin):
    total = spread[192:256, begin + 128 : begin + 640]
    for q in range(3):
        rows = spread[64 * q : 64 * q + 64, begin : begin + 640]
        total = total + pltpu.roll(rows, 96 - 32 * q, 1)[:, 128:]
    return total


def column_of(row):
    diagonal = tile_iota(ATOMS, ATOMS, 0) == tile_iota(ATOMS, ATOMS, 1)
    return jnp.sum(jnp.where(diagonal, jnp.broadcast_to(row, (ATOMS, ATOMS)), 0.0), axis=1, keepdims=True)


def kernel(
    slabs,
    bank,
    codes,
    signal,
    step_size,
    threshold,
    out_codes,
    out_residual,
    natural,
    synthesis,
    gradient,
    lowered,
    own,
    code_shift,
    spread,
    part,
    from_atom,
    from_next,
    misfit,
    misfit_shift,
    grad_send,
    grad_recv,
    code_send,
    scales,
    halo_sems,
    part_send,
    part_recv,
    grad_send_sem,
    grad_recv_sem,
    code_send_sem,
    code_recv_sem,
    edge_send_sem,
    edge_recv_sem,
):
    tm, atom, me = lax.axis_index("tm"), lax.axis_index("atom"), lax.axis_index("chan")
    after, before = lax.rem(tm + 1, slabs), lax.rem(tm + slabs - 1, slabs)
    other = 1 - atom
    my_rows = pl.multiple_of(me // 4 * 16, 16)
    my_block = lax.rem(me, 4)

    barrier = pltpu.get_barrier_semaphore()

    def greet(device):
        pl.semaphore_signal(barrier, 1, device_id=device, device_id_type=MESH)

    def greet_group(turn, carry):
        greet({"chan": lax.rem(me + turn, GROUP)})
        return carry

    def greet_before(turn, carry):
        greet({"tm": before, "chan": lax.rem(me + turn, GROUP)})
        return carry

    greet({"atom": other})
    greet({"tm": after})
    greet({"tm": after, "atom": other})
    lax.fori_loop(0, GROUP, greet_before, 0)
    lax.fori_loop(1, GROUP, greet_group, 0)

    for block in range(8):
        lowered[1 + block // 4, block % 4] = codes[:, 128 * block : 128 * block + 128].astype(BF16)
    arrange_bank(bank, natural, synthesis, gradient)
    scales[:, 0:1] = column_of(step_size[...])
    scales[:, 1:2] = column_of(threshold[...])
    for half in range(2):
        at = pl.multiple_of((my_block + 4 * half) * 128, 128)
        own[half] = codes[pl.ds(my_rows, 16), pl.ds(at, 128)]

    def codes_of(first, last):
        return jnp.concatenate([lowered[b // 4, b % 4] for b in range(first, last)], axis=1)

    def late_half(sweep):
        shift_codes(codes_of(4, 12), 1024, code_shift, 512)
        synthesize(code_shift, synthesis, spread, 512, 1152)
        recon = gather_rows(spread, 512)
        part[sweep, 1] = recon - jnp.where(atom == 0, signal[:, HALF:].astype(F32), 0.0)

    def early_half(sweep):
        edge = jnp.where(tm > 0, codes_of(0, 4).astype(F32), 0.0).astype(BF16)
        shift_codes(jnp.concatenate([edge, lowered[1, 0]], axis=1), 512, code_shift, 0)
        synthesize(code_shift, synthesis, spread, 0, 512)
        recon = gather_rows(spread, 0)
        part[sweep, 0] = recon - jnp.where(atom == 0, signal[:, :HALF].astype(F32), 0.0)

    def part_copy(sweep, index, half, target, device):
        return pltpu.make_async_remote_copy(
            src_ref=part.at[sweep, half],
            dst_ref=target,
            send_sem=part_send.at[sweep, index],
            recv_sem=part_recv.at[sweep, index],
            device_id=device,
            device_id_type=MESH,
        )

    def grad_copy(half, turn):
        owner = lax.rem(me + turn, GROUP)
        return pltpu.make_async_remote_copy(
            src_ref=grad_send.at[half, owner],
            dst_ref=grad_recv.at[half, turn],
            send_sem=grad_send_sem.at[half, turn],
            recv_sem=grad_recv_sem.at[half, turn],
            device_id={"chan": owner},
            device_id_type=MESH,
        )

    def code_place(last, half):
        if last:
            at = pl.multiple_of((my_block + 4 * half) * 128, 128)
            return out_codes.at[pl.ds(my_rows, 16), pl.ds(at, 128)]
        return lowered.at[1 + half, my_block, pl.ds(my_rows, 16)]

    def code_copy(last, half, turn):
        return pltpu.make_async_remote_copy(
            src_ref=own.at[half] if last else code_send.at[half],
            dst_ref=code_place(last, half),
            send_sem=code_send_sem.at[half, turn],
            recv_sem=code_recv_sem.at[half, turn],
            device_id={"chan": lax.rem(me + turn, GROUP)},
            device_id_type=MESH,
        )

    def edge_copy(turn):
        return pltpu.make_async_remote_copy(
            src_ref=code_send.at[1],
            dst_ref=lowered.at[0, my_block, pl.ds(my_rows, 16)],
            send_sem=edge_send_sem.at[turn],
            recv_sem=edge_recv_sem.at[turn],
            device_id={"tm": after, "chan": lax.rem(me + turn, GROUP)},
            device_id_type=MESH,
        )

    def each(first, act):
        def run(turn, carry):
            act(turn)
            return carry

        lax.fori_loop(first, GROUP, run, 0)

    halo = pltpu.make_async_remote_copy(
        src_ref=lowered.at[2],
        dst_ref=lowered.at[0],
        send_sem=halo_sems.at[0],
        recv_sem=halo_sems.at[1],
        device_id={"tm": after},
        device_id_type=MESH,
    )

    for sweep in range(ITERS):
        last = sweep == ITERS - 1
        copies = [
            part_copy(sweep, 0, 1, from_atom.at[sweep, 1], {"atom": other}),
            part_copy(sweep, 1, 0, from_atom.at[sweep, 0], {"atom": other}),
            part_copy(sweep, 2, 0, from_next.at[sweep, 0], {"tm": before}),
            part_copy(sweep, 3, 0, from_next.at[sweep, 1], {"tm": before, "atom": other}),
        ]
        late_half(sweep)
        if sweep == 0:
            pl.semaphore_wait(barrier, 2 * GROUP + 2)
            halo.start()
        copies[0].start()
        if sweep == 0:
            halo.wait()
        else:
            each(0, lambda turn: edge_copy(turn).wait())
        early_half(sweep)
        for copy in (copies[3], copies[2], copies[1]):
            copy.start()

        copies[0].wait_recv()
        whole = part[sweep, 1] + from_atom[sweep, 1]
        misfit[:, HALF:SLAB] = whole
        if last:
            out_residual[:, HALF:SLAB] = whole
        shift_misfit(misfit, 4, 8, 1, misfit_shift)
        copies[1].wait_recv()
        whole = part[sweep, 0] + from_atom[sweep, 0]
        misfit[:, :HALF] = whole
        if last:
            out_residual[:, :HALF] = whole
        shift_misfit(misfit, 0, 5, 0, misfit_shift)
        correlate(misfit_shift, gradient, spread, 0, 640)

        def put(half):
            total = gather_taps(spread, HALF * half)
            for owner in range(GROUP):
                row, block = owner // 4 * 16, owner % 4 * 128
                grad_send[half, owner] = total[row : row + 16, block : block + 128]
            each(1, lambda turn: grad_copy(half, turn).start())

        put(0)
        copies[2].wait_recv()
        copies[3].wait_recv()
        whole = from_next[sweep, 0] + from_next[sweep, 1]
        misfit[:, SLAB:] = jnp.where(tm < slabs - 1, whole, 0.0)
        shift_misfit(misfit, 7, 12, 1, misfit_shift)
        correlate(misfit_shift, gradient, spread, 640, 1152)
        put(1)

        for half in range(2):
            each(1, lambda turn: grad_copy(half, turn).wait_recv())
            total = grad_send[half, me]
            for turn in range(1, GROUP):
                total = total + grad_recv[half, turn]
            step = scales[pl.ds(my_rows, 16), 0:1]
            bound = step * scales[pl.ds(my_rows, 16), 1:2]
            moved = own[half] - step * total
            updated = moved - jnp.clip(moved, -bound, bound)
            own[half] = updated
            if not last:
                code_send[half] = updated.astype(BF16)
            each(1, lambda turn: code_copy(last, half, turn).start())
            if half == 1 and not last:
                each(0, lambda turn: edge_copy(turn).start())
            code_place(last, half)[...] = updated if last else updated.astype(BF16)
        for half in range(2):
            each(1, lambda turn: code_copy(last, half, turn).wait())
            each(1, lambda turn: grad_copy(half, turn).wait_send())
        for copy in copies:
            copy.wait_send()


def body(signal, codes_init, atom_bank, step_size, threshold):
    vmem = pl.BlockSpec(memory_space=pltpu.VMEM)
    return pl.pallas_call(
        functools.partial(kernel, lax.axis_size("tm")),
        out_shape=(
            jax.ShapeDtypeStruct((ATOMS, SLAB), F32),
            jax.ShapeDtypeStruct((CHANS, SLAB), F32),
        ),
        in_specs=[vmem] * 5,
        out_specs=(vmem, vmem),
        scratch_shapes=[
            pltpu.VMEM((256, 2048), BF16),
            pltpu.VMEM((256, 2048), BF16),
            pltpu.VMEM((256, 2048), BF16),
            pltpu.VMEM((3, 4, ATOMS, LANES), BF16),
            pltpu.VMEM((2, 16, LANES), F32),
            pltpu.VMEM((8, ATOMS, 1536), BF16),
            pltpu.VMEM((256, 1152), F32),
            pltpu.VMEM((ITERS, 2, CHANS, HALF), F32),
            pltpu.VMEM((ITERS, 2, CHANS, HALF), F32),
            pltpu.VMEM((ITERS, 2, CHANS, HALF), F32),
            pltpu.VMEM((CHANS, 1536), F32),
            pltpu.VMEM((4, 128, 1536), BF16),
            pltpu.VMEM((2, GROUP, 16, LANES), F32),
            pltpu.VMEM((2, GROUP, 16, LANES), F32),
            pltpu.VMEM((2, 16, LANES), BF16),
            pltpu.VMEM((ATOMS, LANES), F32),
            pltpu.SemaphoreType.DMA((2,)),
            pltpu.SemaphoreType.DMA((ITERS, 4)),
            pltpu.SemaphoreType.DMA((ITERS, 4)),
            pltpu.SemaphoreType.DMA((2, GROUP)),
            pltpu.SemaphoreType.DMA((2, GROUP)),
            pltpu.SemaphoreType.DMA((2, GROUP)),
            pltpu.SemaphoreType.DMA((2, GROUP)),
            pltpu.SemaphoreType.DMA((GROUP,)),
            pltpu.SemaphoreType.DMA((GROUP,)),
        ],
        compiler_params=pltpu.CompilerParams(
            collective_id=0, has_side_effects=True, vmem_limit_bytes=48 * 1024 * 1024
        ),
    )(
        atom_bank.reshape(ATOMS * CHANS, TAPS),
        codes_init,
        signal,
        step_size.reshape(1, ATOMS),
        threshold.reshape(1, ATOMS),
    )


def solution(mesh):
    placed = (P("chan", "tm"), P("atom", "tm"), P("atom", "chan", None), P("atom"), P("atom"))
    return jax.shard_map(
        body,
        mesh=mesh,
        in_specs=placed,
        out_specs=(P("atom", "tm"), P("chan", "tm")),
        check_vma=False,
    )
```

time: 1400 us -> 57.2 us (0.04)
  local copies, waits for them, and re-layouts: 876 us -> 4.92 us
  waiting for transfers between devices: 364 us -> 0 us
  matrix products: 129 us -> 0 us
  Pallas kernels: 0 us -> 51.4 us
    while x1984 -> x0, local copies, waits for them, and re-layouts: 836 us -> none
    psum x4 -> x0, waiting for transfers between devices: 360 us -> none  [the longest x2 290 us: body(): gradient = lax.psum(partial_grad, 'chan')]
    dot_general x64 -> x0, matrix products: 129 us -> none  [the longest x32 92.1 us: synthesize_accumulate(): jnp.dot(weights[turn_index], stacked, preferred_element_type=jnp.float32)]
    pallas_call x0 -> x1, Pallas kernels: none -> 51.4 us  [body(): pl.pallas_call(functools.partial(kernel, lax.axis_size('tm')), out_shape=...]
    concatenate x64 -> x0, local copies, waits for them, and re-layouts: 26.9 us -> none  [the longest x32 24.3 us: synthesize_accumulate(): jnp.concatenate([window[:, group - 1 - offset:group - 1 - offset + length...]
  transfers between devices with their start and end apart: 8 -> 0, of which waited for: 6 -> 0; matrix products, arithmetic and copies ran while one was open for 1% -> 0% of each run, Pallas kernels for 0% -> 0%
where the time goes in v1:
time: 57.2 us; the launch traced here: 57 us
  Pallas kernels  51.4 us (90%)
  local copies, waits for them, and re-layouts  4.92 us (9%)
  between operations  0.66 us (1%)
    pallas_call x1, Pallas kernels, body(): pl.pallas_call(functools.partial(kernel, lax.axis_size('tm')), out_shape=...  51.4 us
    unnamed x12, local copies, waits for them, and re-layouts  4.92 us

profile of v1, /device:TPU:1, one launch (start us, length us, event | category | flops | bytes accessed | tf_op | source)
XLA Modules:
  0.0 57.0 jit_solution(9438916162116946321)
XLA Ops:
  0.6 0.0 copy-start.3
  0.6 0.0 copy-start.4
  0.7 0.6 %copy-done.3 = f32[64]{0:T(128)S(1)} copy-done((f32[64]{0:T(128)S(1)}, f32[64]{0:T(128)}, u32[]{:S(2)}) %copy-start.3) | copy-done | bytes 280
  1.3 0.0 copy-done.4
  1.3 0.0 copy-start
  1.3 1.2 %copy-done = bf16[64,16,512]{2,1,0:T(8,128)(2,1)S(1)} copy-done((bf16[64,16,512]{2,1,0:T(8,128)(2,1)S(1)}, bf16[64,16,512]{2,1,0:T(8,128)(2,1)}, u32[]{:S(2)}) %copy-start) | copy-done | bytes 1048600
  2.5 0.0 copy-start.1
  2.5 0.9 %copy-done.1 = f32[64,1024]{1,0:T(8,128)S(1)} copy-done((f32[64,1024]{1,0:T(8,128)S(1)}, f32[64,1024]{1,0:T(8,128)}, u32[]{:S(2)}) %copy-start.1) | copy-done | bytes 262168
  3.5 0.0 copy-start.2
  3.5 0.8 %copy-done.2 = bf16[16,1024]{1,0:T(8,128)(2,1)S(1)} copy-done((bf16[16,1024]{1,0:T(8,128)(2,1)S(1)}, bf16[16,1024]{1,0:T(8,128)(2,1)}, u32[]{:S(2)}) %copy-start.2) | copy-done | bytes 32792
  4.2 51.4 %shard_map.68 = (f32[64,1024]{1,0:T(8,128)S(1)}, f32[16,1024]{1,0:T(8,128)S(1)}) custom-call(bf16[1024,512]{1,0:T(8,128)(2,1)S(1)} %bitcast.3, f32[64,1024]{1,0:T(8,128)S(1)} %copy-done.1, bf16[16,1024]{1,0:T(8,128)(2,1)S(1)} %copy-done.2, f32[1,64]{1,0:T(1,128)S(1)} %bitcast.4, f32[1,64]{1,0:T(1,128)S(1)} %bitcast.5), custom_call_target="tpu_custom_call" | custom-call | tf_op jit(solution)/shard_map/pallas_call | solution.py:360
  55.6 0.7 %copy.9 = f32[64,1024]{1,0:T(8,128)} copy(f32[64,1024]{1,0:T(8,128)S(1)} %get-tuple-element.4) | data formatting | bytes 524288
  56.3 0.6 %copy.10 = f32[16,1024]{1,0:T(8,128)} copy(f32[16,1024]{1,0:T(8,128)S(1)} %get-tuple-element.5) | data formatting | bytes 131072
Async XLA Ops:
  0.6 0.7 %copy-start.3 = (f32[64]{0:T(128)S(1)}, f32[64]{0:T(128)}, u32[]{:S(2)}) copy-start(f32[64]{0:T(128)} %param.8) | copy-start | bytes 772
  0.6 0.7 %copy-start.4 = (f32[64]{0:T(128)S(1)}, f32[64]{0:T(128)}, u32[]{:S(2)}) copy-start(f32[64]{0:T(128)} %param.9) | copy-start | bytes 772
  1.3 1.2 %copy-start = (bf16[64,16,512]{2,1,0:T(8,128)(2,1)S(1)}, bf16[64,16,512]{2,1,0:T(8,128)(2,1)}, u32[]{:S(2)}) copy-start(bf16[64,16,512]{2,1,0:T(8,128)(2,1)} %param.7) | copy-start | bytes 3145732
  2.5 0.9 %copy-start.1 = (f32[64,1024]{1,0:T(8,128)S(1)}, f32[64,1024]{1,0:T(8,128)}, u32[]{:S(2)}) copy-start(f32[64,1024]{1,0:T(8,128)} %codes.1) | copy-start | bytes 786436
  3.5 0.8 %copy-start.2 = (bf16[16,1024]{1,0:T(8,128)(2,1)S(1)}, bf16[16,1024]{1,0:T(8,128)(2,1)}, u32[]{:S(2)}) copy-start(bf16[16,1024]{1,0:T(8,128)(2,1)} %signal.1) | copy-start | bytes 98308

commit v2 on v1

--- a/solution.py
+++ b/solution.py
@@ -135,13 +135,18 @@
 
 def kernel(
     slabs,
+    bank_hbm,
+    codes_hbm,
+    signal_hbm,
+    step_size_hbm,
+    threshold_hbm,
+    out_codes,
+    out_residual,
     bank,
     codes,
     signal,
     step_size,
     threshold,
-    out_codes,
-    out_residual,
     natural,
     synthesis,
     gradient,
@@ -167,6 +172,8 @@
     code_recv_sem,
     edge_send_sem,
     edge_recv_sem,
+    load_sems,
+    word,
 ):
     tm, atom, me = lax.axis_index("tm"), lax.axis_index("atom"), lax.axis_index("chan")
     after, before = lax.rem(tm + 1, slabs), lax.rem(tm + slabs - 1, slabs)
@@ -176,25 +183,59 @@
 
     barrier = pltpu.get_barrier_semaphore()
 
-    def greet(device):
-        pl.semaphore_signal(barrier, 1, device_id=device, device_id_type=MESH)
-
-    def greet_group(turn, carry):
-        greet({"chan": lax.rem(me + turn, GROUP)})
-        return carry
-
-    def greet_before(turn, carry):
-        greet({"tm": before, "chan": lax.rem(me + turn, GROUP)})
-        return carry
-
-    greet({"atom": other})
-    greet({"tm": after})
-    greet({"tm": after, "atom": other})
-    lax.fori_loop(0, GROUP, greet_before, 0)
-    lax.fori_loop(1, GROUP, greet_group, 0)
-
+    def near(signal_one):
+        for device in (
+            {"tm": after},
+            {"tm": before},
+            {"atom": other},
+            {"chan": me + 1 - 2 * lax.rem(me, 2)},
+            {"chan": me + 2 - 4 * lax.rem(me // 2, 2)},
+            {"chan": lax.rem(me + 4, GROUP)},
+            {"chan": lax.rem(me + 8, GROUP)},
+            {"chan": lax.rem(me + 12, GROUP)},
+        ):
+            signal_one(device)
+
+    near(lambda device: pl.semaphore_signal(barrier, 1, device_id=device, device_id_type=MESH))
+    loads = [
+        pltpu.make_async_copy(source, target, load_sems.at[index])
+        for index, (source, target) in enumerate(
+            (
+                (codes_hbm, codes),
+                (bank_hbm, bank),
+                (signal_hbm, signal),
+                (step_size_hbm, step_size),
+                (threshold_hbm, threshold),
+            )
+        )
+    ]
+    for load in loads:
+        load.start()
+
+    def spread_word(stage):
+        near(
+            lambda device: pl.semaphore_signal(
+                word.at[stage], 1, device_id=device, device_id_type=MESH
+            )
+        )
+
+    halo = pltpu.make_async_remote_copy(
+        src_ref=lowered.at[2],
+        dst_ref=lowered.at[0],
+        send_sem=halo_sems.at[0],
+        recv_sem=halo_sems.at[1],
+        device_id={"tm": after},
+        device_id_type=MESH,
+    )
+
+    loads[0].wait()
     for block in range(8):
         lowered[1 + block // 4, block % 4] = codes[:, 128 * block : 128 * block + 128].astype(BF16)
+    for load in loads[1:]:
+        load.wait()
+    pl.semaphore_wait(barrier, 8)
+    spread_word(0)
+    halo.start()
     arrange_bank(bank, natural, synthesis, gradient)
     scales[:, 0:1] = column_of(step_size[...])
     scales[:, 1:2] = column_of(threshold[...])
@@ -272,15 +313,6 @@
 
         lax.fori_loop(first, GROUP, run, 0)
 
-    halo = pltpu.make_async_remote_copy(
-        src_ref=lowered.at[2],
-        dst_ref=lowered.at[0],
-        send_sem=halo_sems.at[0],
-        recv_sem=halo_sems.at[1],
-        device_id={"tm": after},
-        device_id_type=MESH,
-    )
-
     for sweep in range(ITERS):
         last = sweep == ITERS - 1
         copies = [
@@ -290,12 +322,11 @@
             part_copy(sweep, 3, 0, from_next.at[sweep, 1], {"tm": before, "atom": other}),
         ]
         late_half(sweep)
-        if sweep == 0:
-            pl.semaphore_wait(barrier, 2 * GROUP + 2)
-            halo.start()
         copies[0].start()
         if sweep == 0:
             halo.wait()
+            pl.semaphore_wait(word.at[0], 8)
+            spread_word(1)
         else:
             each(0, lambda turn: edge_copy(turn).wait())
         early_half(sweep)
@@ -321,6 +352,9 @@
             for owner in range(GROUP):
                 row, block = owner // 4 * 16, owner % 4 * 128
                 grad_send[half, owner] = total[row : row + 16, block : block + 128]
+            if sweep == 0 and half == 0:
+                pl.semaphore_wait(word.at[1], 8)
+                spread_word(2)
             each(1, lambda turn: grad_copy(half, turn).start())
 
         put(0)
@@ -346,6 +380,7 @@
                 code_send[half] = updated.astype(BF16)
             each(1, lambda turn: code_copy(last, half, turn).start())
             if half == 1 and not last:
+                pl.semaphore_wait(word.at[2], 8)
                 each(0, lambda turn: edge_copy(turn).start())
             code_place(last, half)[...] = updated if last else updated.astype(BF16)
         for half in range(2):
@@ -363,9 +398,14 @@
             jax.ShapeDtypeStruct((ATOMS, SLAB), F32),
             jax.ShapeDtypeStruct((CHANS, SLAB), F32),
         ),
-        in_specs=[vmem] * 5,
+        in_specs=[pl.BlockSpec(memory_space=pltpu.HBM)] * 5,
         out_specs=(vmem, vmem),
         scratch_shapes=[
+            pltpu.VMEM((ATOMS * CHANS, TAPS), BF16),
+            pltpu.VMEM((ATOMS, SLAB), F32),
+            pltpu.VMEM((CHANS, SLAB), BF16),
+            pltpu.VMEM((1, ATOMS), F32),
+            pltpu.VMEM((1, ATOMS), F32),
             pltpu.VMEM((256, 2048), BF16),
             pltpu.VMEM((256, 2048), BF16),
             pltpu.VMEM((256, 2048), BF16),
@@ -391,16 +431,23 @@
             pltpu.SemaphoreType.DMA((2, GROUP)),
             pltpu.SemaphoreType.DMA((GROUP,)),
             pltpu.SemaphoreType.DMA((GROUP,)),
+            pltpu.SemaphoreType.DMA((5,)),
+            pltpu.SemaphoreType.REGULAR((3,)),
         ],
         compiler_params=pltpu.CompilerParams(
             collective_id=0, has_side_effects=True, vmem_limit_bytes=48 * 1024 * 1024
         ),
     )(
-        atom_bank.reshape(ATOMS * CHANS, TAPS),
-        codes_init,
-        signal,
-        step_size.reshape(1, ATOMS),
-        threshold.reshape(1, ATOMS),
+        *(
+            pltpu.with_memory_space_constraint(value, pltpu.HBM)
+            for value in (
+                atom_bank.reshape(ATOMS * CHANS, TAPS),
+                codes_init,
+                signal,
+                step_size.reshape(1, ATOMS),
+                threshold.reshape(1, ATOMS),
+            )
+        )
     )
 
 

time: 57.2 us -> 52.3 us (0.914)
  local copies, waits for them, and re-layouts: 4.92 us -> 1.33 us
  Pallas kernels: 51.4 us -> 50.2 us
    unnamed x12 -> x2, local copies, waits for them, and re-layouts: 4.92 us -> 1.33 us
    pallas_call x1, Pallas kernels: 51.4 us -> 50.2 us  [body(): pl.pallas_call(functools.partial(kernel, lax.axis_size('tm')), out_shape=...]
where the time goes in v2:
time: 52.3 us; the launch traced here: 52.2 us
  Pallas kernels  50.2 us (96%)
  local copies, waits for them, and re-layouts  1.33 us (3%)
  between operations  0.64 us (1%)
    pallas_call x1, Pallas kernels, body(): pl.pallas_call(functools.partial(kernel, lax.axis_size('tm')), out_shape=...  50.2 us
    unnamed x2, local copies, waits for them, and re-layouts  1.33 us

profile of v2, /device:TPU:1, one launch (start us, length us, event | category | flops | bytes accessed | tf_op | source)
XLA Modules:
  0.0 52.2 jit_solution(1596979170304487672)
XLA Ops:
  0.6 50.2 %shard_map.68 = (f32[64,1024]{1,0:T(8,128)S(1)}, f32[16,1024]{1,0:T(8,128)S(1)}) custom-call(bf16[1024,512]{1,0:T(8,128)(2,1)} %bitcast.3, f32[64,1024]{1,0:T(8,128)} %codes_hbm.1, bf16[16,1024]{1,0:T(8,128)(2,1)} %signal_hbm.1, f32[1,64]{1,0:T(1,128)} %bitcast.4, f32[1,64]{1,0:T(1,128)} %bitcast.5), custom_call_target="tpu_custom_call" | custom-call | tf_op jit(solution)/shard_map/pallas_call | solution.py:395
  50.8 0.7 %copy.9 = f32[64,1024]{1,0:T(8,128)} copy(f32[64,1024]{1,0:T(8,128)S(1)} %get-tuple-element.4) | data formatting | bytes 524288
  51.5 0.6 %copy.10 = f32[16,1024]{1,0:T(8,128)} copy(f32[16,1024]{1,0:T(8,128)S(1)} %get-tuple-element.5) | data formatting | bytes 131072

commit v3 on v2

--- a/solution.py
+++ b/solution.py
@@ -12,6 +12,7 @@
 ITERS = 2
 ATOMS, CHANS, TAPS, SLAB = 64, 16, 512, 1024
 LANES, HALF = 128, 512
+GRAD_SCALE, CODE_SCALE = 2.0**-8, 2.0**-12
 GROUP = 16
 
 
@@ -126,6 +127,17 @@
         rows = spread[64 * q : 64 * q + 64, begin : begin + 640]
         total = total + pltpu.roll(rows, 96 - 32 * q, 1)[:, 128:]
     return total
+
+
+def encode(value, scale):
+    scaled = value * scale
+    return (scaled * scaled * scaled * jnp.abs(scaled)).astype(BF16)
+
+
+def decode(code, scale):
+    power = code.astype(F32)
+    root = jnp.sqrt(jnp.sqrt(jnp.abs(power))) * (1.0 / scale)
+    return jnp.where(power < 0.0, -root, root)
 
 
 def column_of(row):
@@ -178,15 +190,23 @@
     tm, atom, me = lax.axis_index("tm"), lax.axis_index("atom"), lax.axis_index("chan")
     after, before = lax.rem(tm + 1, slabs), lax.rem(tm + slabs - 1, slabs)
     other = 1 - atom
+    has_before, has_after = tm > 0, tm < slabs - 1
+    near_count = 6 + has_before.astype(jnp.int32) + has_after.astype(jnp.int32)
     my_rows = pl.multiple_of(me // 4 * 16, 16)
     my_block = lax.rem(me, 4)
 
     barrier = pltpu.get_barrier_semaphore()
 
     def near(signal_one):
+        @pl.when(has_after)
+        def _():
+            signal_one({"tm": after})
+
+        @pl.when(has_before)
+        def _():
+            signal_one({"tm": before})
+
         for device in (
-            {"tm": after},
-            {"tm": before},
             {"atom": other},
             {"chan": me + 1 - 2 * lax.rem(me, 2)},
             {"chan": me + 2 - 4 * lax.rem(me // 2, 2)},
@@ -228,14 +248,22 @@
         device_id_type=MESH,
     )
 
+    @pl.when(jnp.logical_not(has_before))
+    def _():
+        lowered[0] = jnp.zeros_like(lowered[0])
+
+    @pl.when(jnp.logical_not(has_after))
+    def _():
+        from_next[...] = jnp.zeros_like(from_next)
+
     loads[0].wait()
     for block in range(8):
         lowered[1 + block // 4, block % 4] = codes[:, 128 * block : 128 * block + 128].astype(BF16)
     for load in loads[1:]:
         load.wait()
-    pl.semaphore_wait(barrier, 8)
+    pl.semaphore_wait(barrier, near_count)
     spread_word(0)
-    halo.start()
+    pl.when(has_after)(halo.start)
     arrange_bank(bank, natural, synthesis, gradient)
     scales[:, 0:1] = column_of(step_size[...])
     scales[:, 1:2] = column_of(threshold[...])
@@ -253,8 +281,7 @@
         part[sweep, 1] = recon - jnp.where(atom == 0, signal[:, HALF:].astype(F32), 0.0)
 
     def early_half(sweep):
-        edge = jnp.where(tm > 0, codes_of(0, 4).astype(F32), 0.0).astype(BF16)
-        shift_codes(jnp.concatenate([edge, lowered[1, 0]], axis=1), 512, code_shift, 0)
+        shift_codes(codes_of(0, 5), 512, code_shift, 0)
         synthesize(code_shift, synthesis, spread, 0, 512)
         recon = gather_rows(spread, 0)
         part[sweep, 0] = recon - jnp.where(atom == 0, signal[:, :HALF].astype(F32), 0.0)
@@ -288,7 +315,7 @@
 
     def code_copy(last, half, turn):
         return pltpu.make_async_remote_copy(
-            src_ref=own.at[half] if last else code_send.at[half],
+            src_ref=code_send.at[half],
             dst_ref=code_place(last, half),
             send_sem=code_send_sem.at[half, turn],
             recv_sem=code_recv_sem.at[half, turn],
@@ -324,14 +351,16 @@
         late_half(sweep)
         copies[0].start()
         if sweep == 0:
-            halo.wait()
-            pl.semaphore_wait(word.at[0], 8)
+            pl.when(has_before)(halo.wait_recv)
+            pl.when(has_after)(halo.wait_send)
+            pl.semaphore_wait(word.at[0], near_count)
             spread_word(1)
         else:
-            each(0, lambda turn: edge_copy(turn).wait())
+            pl.when(has_before)(lambda: each(0, lambda turn: edge_copy(turn).wait_recv()))
         early_half(sweep)
-        for copy in (copies[3], copies[2], copies[1]):
-            copy.start()
+        pl.when(has_before)(copies[3].start)
+        pl.when(has_before)(copies[2].start)
+        copies[1].start()
 
         copies[0].wait_recv()
         whole = part[sweep, 1] + from_atom[sweep, 1]
@@ -351,51 +380,54 @@
             total = gather_taps(spread, HALF * half)
             for owner in range(GROUP):
                 row, block = owner // 4 * 16, owner % 4 * 128
-                grad_send[half, owner] = total[row : row + 16, block : block + 128]
+                piece = total[row : row + 16, block : block + 128]
+                grad_send[half, owner] = encode(piece, GRAD_SCALE)
             if sweep == 0 and half == 0:
-                pl.semaphore_wait(word.at[1], 8)
+                pl.semaphore_wait(word.at[1], near_count)
                 spread_word(2)
             each(1, lambda turn: grad_copy(half, turn).start())
 
         put(0)
-        copies[2].wait_recv()
-        copies[3].wait_recv()
-        whole = from_next[sweep, 0] + from_next[sweep, 1]
-        misfit[:, SLAB:] = jnp.where(tm < slabs - 1, whole, 0.0)
+        pl.when(has_after)(copies[2].wait_recv)
+        pl.when(has_after)(copies[3].wait_recv)
+        misfit[:, SLAB:] = from_next[sweep, 0] + from_next[sweep, 1]
         shift_misfit(misfit, 7, 12, 1, misfit_shift)
         correlate(misfit_shift, gradient, spread, 640, 1152)
         put(1)
 
         for half in range(2):
             each(1, lambda turn: grad_copy(half, turn).wait_recv())
-            total = grad_send[half, me]
+            total = decode(grad_send[half, me], GRAD_SCALE)
             for turn in range(1, GROUP):
-                total = total + grad_recv[half, turn]
+                total = total + decode(grad_recv[half, turn], GRAD_SCALE)
             step = scales[pl.ds(my_rows, 16), 0:1]
             bound = step * scales[pl.ds(my_rows, 16), 1:2]
             moved = own[half] - step * total
             updated = moved - jnp.clip(moved, -bound, bound)
             own[half] = updated
-            if not last:
-                code_send[half] = updated.astype(BF16)
+            code_send[half] = encode(updated, CODE_SCALE) if last else updated.astype(BF16)
             each(1, lambda turn: code_copy(last, half, turn).start())
             if half == 1 and not last:
-                pl.semaphore_wait(word.at[2], 8)
-                each(0, lambda turn: edge_copy(turn).start())
-            code_place(last, half)[...] = updated if last else updated.astype(BF16)
+                pl.semaphore_wait(word.at[2], near_count)
+                pl.when(has_after)(lambda: each(0, lambda turn: edge_copy(turn).start()))
+            code_place(last, half)[...] = code_send[half]
         for half in range(2):
             each(1, lambda turn: code_copy(last, half, turn).wait())
             each(1, lambda turn: grad_copy(half, turn).wait_send())
-        for copy in copies:
-            copy.wait_send()
+        if not last:
+            pl.when(has_after)(lambda: each(0, lambda turn: edge_copy(turn).wait_send()))
+        copies[0].wait_send()
+        copies[1].wait_send()
+        pl.when(has_before)(copies[2].wait_send)
+        pl.when(has_before)(copies[3].wait_send)
 
 
 def body(signal, codes_init, atom_bank, step_size, threshold):
     vmem = pl.BlockSpec(memory_space=pltpu.VMEM)
-    return pl.pallas_call(
+    coded, residual = pl.pallas_call(
         functools.partial(kernel, lax.axis_size("tm")),
         out_shape=(
-            jax.ShapeDtypeStruct((ATOMS, SLAB), F32),
+            jax.ShapeDtypeStruct((ATOMS, SLAB), BF16),
             jax.ShapeDtypeStruct((CHANS, SLAB), F32),
         ),
         in_specs=[pl.BlockSpec(memory_space=pltpu.HBM)] * 5,
@@ -418,8 +450,8 @@
             pltpu.VMEM((ITERS, 2, CHANS, HALF), F32),
             pltpu.VMEM((CHANS, 1536), F32),
             pltpu.VMEM((4, 128, 1536), BF16),
-            pltpu.VMEM((2, GROUP, 16, LANES), F32),
-            pltpu.VMEM((2, GROUP, 16, LANES), F32),
+            pltpu.VMEM((2, GROUP, 16, LANES), BF16),
+            pltpu.VMEM((2, GROUP, 16, LANES), BF16),
             pltpu.VMEM((2, 16, LANES), BF16),
             pltpu.VMEM((ATOMS, LANES), F32),
             pltpu.SemaphoreType.DMA((2,)),
@@ -449,6 +481,7 @@
             )
         )
     )
+    return decode(coded, CODE_SCALE), residual
 
 
 def solution(mesh):

time: 52.3 us -> 46 us (0.88)
  Pallas kernels: 50.2 us -> 43.5 us
  other arithmetic: 0 us -> 0.88 us
  local copies, waits for them, and re-layouts: 1.33 us -> 0.63 us
    pallas_call x1, Pallas kernels: 50.2 us -> 43.5 us  [body(): pl.pallas_call(functools.partial(kernel, lax.axis_size('tm')), out_shape=...]
    select_n x0 -> x1, other arithmetic: none -> 0.88 us  [decode(): return jnp.where(power < 0.0, -root, root)]
    unnamed x2 -> x1, local copies, waits for them, and re-layouts: 1.33 us -> 0.63 us
where the time goes in v3:
time: 46 us; the launch traced here: 45.6 us
  Pallas kernels  43.5 us (95%)
  other arithmetic  0.88 us (2%)
  between operations  0.64 us (1%)
  local copies, waits for them, and re-layouts  0.63 us (1%)
    pallas_call x1, Pallas kernels, body(): pl.pallas_call(functools.partial(kernel, lax.axis_size('tm')), out_shape=...  43.5 us

profile of v3, /device:TPU:1, one launch (start us, length us, event | category | flops | bytes accessed | tf_op | source)
XLA Modules:
  0.0 45.6 jit_solution(8543007947330720516)
XLA Ops:
  0.6 43.5 %shard_map.68 = (bf16[64,1024]{1,0:T(8,128)(2,1)S(1)}, f32[16,1024]{1,0:T(8,128)S(1)}) custom-call(bf16[1024,512]{1,0:T(8,128)(2,1)} %bitcast.3, f32[64,1024]{1,0:T(8,128)} %codes_hbm.1, bf16[16,1024]{1,0:T(8,128)(2,1)} %signal_hbm.1, f32[1,64]{1,0:T(1,128)} %bitcast.4, f32[1,64]{1,0:T(1,128)} %bitcast.5), custom_call_target="tpu_custom_call" | custom-call | tf_op jit(solution)/shard_map/pallas_call | solution.py:427
  44.1 0.9 %negate_select_fusion = f32[64,1024]{1,0:T(8,128)} fusion(bf16[64,1024]{1,0:T(8,128)(2,1)S(1)} %get-tuple-element.4), kind=kLoop, calls=%fused_computation | loop fusion | flops 393216 | bytes 393216 | tf_op jit(solution)/shard_map/jit(_where)/select_n | solution.py:140
  45.0 0.6 %copy.8 = f32[16,1024]{1,0:T(8,128)} copy(f32[16,1024]{1,0:T(8,128)S(1)} %get-tuple-element.9) | data formatting | bytes 131072

commit v4 on v3

--- a/solution.py
+++ b/solution.py
@@ -14,6 +14,7 @@
 LANES, HALF = 128, 512
 GRAD_SCALE, CODE_SCALE = 2.0**-8, 2.0**-12
 GROUP = 16
+STEPS = [(y, x, core) for y, x in ((2, 1), (1, 1), (3, 1), (2, 0), (0, 1), (1, 0), (3, 0), (0, 0)) for core in (1, 0)]
 
 
 def tile_iota(rows, columns, dimension):
@@ -195,6 +196,15 @@
     my_rows = pl.multiple_of(me // 4 * 16, 16)
     my_block = lax.rem(me, 4)
 
+    def at_step(step):
+        y, x, core = step
+        return (
+            lax.rem(me // 4 + y, 4) * 4 + lax.rem(me // 2 + x, 2) * 2 + lax.rem(me + core, 2)
+        )
+
+    def slot(step):
+        return step[0] * 4 + step[1] * 2 + step[2]
+
     barrier = pltpu.get_barrier_semaphore()
 
     def near(signal_one):
@@ -296,13 +306,13 @@
             device_id_type=MESH,
         )
 
-    def grad_copy(half, turn):
-        owner = lax.rem(me + turn, GROUP)
+    def grad_copy(half, step):
+        owner = at_step(step)
         return pltpu.make_async_remote_copy(
             src_ref=grad_send.at[half, owner],
-            dst_ref=grad_recv.at[half, turn],
-            send_sem=grad_send_sem.at[half, turn],
-            recv_sem=grad_recv_sem.at[half, turn],
+            dst_ref=grad_recv.at[half, slot(step)],
+            send_sem=grad_send_sem.at[half],
+            recv_sem=grad_recv_sem.at[half],
             device_id={"chan": owner},
             device_id_type=MESH,
         )
@@ -313,33 +323,37 @@
             return out_codes.at[pl.ds(my_rows, 16), pl.ds(at, 128)]
         return lowered.at[1 + half, my_block, pl.ds(my_rows, 16)]
 
-    def code_copy(last, half, turn):
+    def code_copy(last, half, step):
         return pltpu.make_async_remote_copy(
             src_ref=code_send.at[half],
             dst_ref=code_place(last, half),
-            send_sem=code_send_sem.at[half, turn],
-            recv_sem=code_recv_sem.at[half, turn],
-            device_id={"chan": lax.rem(me + turn, GROUP)},
+            send_sem=code_send_sem.at[half],
+            recv_sem=code_recv_sem.at[half],
+            device_id={"chan": at_step(step)},
             device_id_type=MESH,
         )
 
-    def edge_copy(turn):
+    def edge_copy(step):
         return pltpu.make_async_remote_copy(
             src_ref=code_send.at[1],
             dst_ref=lowered.at[0, my_block, pl.ds(my_rows, 16)],
-            send_sem=edge_send_sem.at[turn],
-            recv_sem=edge_recv_sem.at[turn],
-            device_id={"tm": after, "chan": lax.rem(me + turn, GROUP)},
+            send_sem=edge_send_sem,
+            recv_sem=edge_recv_sem,
+            device_id={"tm": after, "chan": at_step(step)},
             device_id_type=MESH,
         )
 
-    def each(first, act):
-        def run(turn, carry):
-            act(turn)
-            return carry
-
-        lax.fori_loop(first, GROUP, run, 0)
-
+    others = [step for step in STEPS if slot(step)]
+
+    def wait_pieces(sem, first):
+        pieces = grad_recv.at[0, first:]
+        pltpu.make_async_copy(pieces, pieces, sem).wait()
+
+    def send_edges():
+        for step in STEPS:
+            edge_copy(step).start()
+
+    sent = []
     for sweep in range(ITERS):
         last = sweep == ITERS - 1
         copies = [
@@ -350,13 +364,14 @@
         ]
         late_half(sweep)
         copies[0].start()
+        sent.extend(copies)
         if sweep == 0:
             pl.when(has_before)(halo.wait_recv)
             pl.when(has_after)(halo.wait_send)
             pl.semaphore_wait(word.at[0], near_count)
             spread_word(1)
         else:
-            pl.when(has_before)(lambda: each(0, lambda turn: edge_copy(turn).wait_recv()))
+            pl.when(has_before)(lambda: wait_pieces(edge_recv_sem, 0))
         early_half(sweep)
         pl.when(has_before)(copies[3].start)
         pl.when(has_before)(copies[2].start)
@@ -378,6 +393,8 @@
 
         def put(half):
             total = gather_taps(spread, HALF * half)
+            if last:
+                wait_pieces(grad_send_sem.at[half], 1)
             for owner in range(GROUP):
                 row, block = owner // 4 * 16, owner % 4 * 128
                 piece = total[row : row + 16, block : block + 128]
@@ -385,7 +402,8 @@
             if sweep == 0 and half == 0:
                 pl.semaphore_wait(word.at[1], near_count)
                 spread_word(2)
-            each(1, lambda turn: grad_copy(half, turn).start())
+            for step in others:
+                grad_copy(half, step).start()
 
         put(0)
         pl.when(has_after)(copies[2].wait_recv)
@@ -396,7 +414,7 @@
         put(1)
 
         for half in range(2):
-            each(1, lambda turn: grad_copy(half, turn).wait_recv())
+            wait_pieces(grad_recv_sem.at[half], 1)
             total = decode(grad_send[half, me], GRAD_SCALE)
             for turn in range(1, GROUP):
                 total = total + decode(grad_recv[half, turn], GRAD_SCALE)
@@ -405,21 +423,40 @@
             moved = own[half] - step * total
             updated = moved - jnp.clip(moved, -bound, bound)
             own[half] = updated
+            if last:
+                wait_pieces(code_send_sem.at[half], 1)
+                if half == 1:
+                    pl.when(has_after)(lambda: wait_pieces(edge_send_sem, 0))
             code_send[half] = encode(updated, CODE_SCALE) if last else updated.astype(BF16)
-            each(1, lambda turn: code_copy(last, half, turn).start())
+            for step in others:
+                code_copy(last, half, step).start()
             if half == 1 and not last:
                 pl.semaphore_wait(word.at[2], near_count)
-                pl.when(has_after)(lambda: each(0, lambda turn: edge_copy(turn).start()))
+                pl.when(has_after)(send_edges)
             code_place(last, half)[...] = code_send[half]
         for half in range(2):
-            each(1, lambda turn: code_copy(last, half, turn).wait())
-            each(1, lambda turn: grad_copy(half, turn).wait_send())
-        if not last:
-            pl.when(has_after)(lambda: each(0, lambda turn: edge_copy(turn).wait_send()))
-        copies[0].wait_send()
-        copies[1].wait_send()
-        pl.when(has_before)(copies[2].wait_send)
-        pl.when(has_before)(copies[3].wait_send)
+            wait_pieces(code_recv_sem.at[half], 1)
+        if last:
+            for half in range(2):
+                wait_pieces(code_send_sem.at[half], 1)
+                wait_pieces(grad_send_sem.at[half], 1)
+            for index, copy in enumerate(sent):
+                if index % 4 < 2:
+                    copy.wait_send()
+                else:
+                    pl.when(has_before)(copy.wait_send)
+
+
+def write_out(coded, residual, out_codes, out_residual, plain, sems):
+    copies = [pltpu.make_async_copy(residual, out_residual, sems.at[4])]
+    copies[0].start()
+    for part in range(4):
+        rows = pl.ds(16 * part, 16)
+        plain[rows, :] = decode(coded[rows, :], CODE_SCALE)
+        copies.append(pltpu.make_async_copy(plain.at[rows], out_codes.at[rows], sems.at[part]))
+        copies[-1].start()
+    for copy in copies:
+        copy.wait()
 
 
 def body(signal, codes_init, atom_bank, step_size, threshold):
@@ -457,12 +494,12 @@
             pltpu.SemaphoreType.DMA((2,)),
             pltpu.SemaphoreType.DMA((ITERS, 4)),
             pltpu.SemaphoreType.DMA((ITERS, 4)),
-            pltpu.SemaphoreType.DMA((2, GROUP)),
-            pltpu.SemaphoreType.DMA((2, GROUP)),
-            pltpu.SemaphoreType.DMA((2, GROUP)),
-            pltpu.SemaphoreType.DMA((2, GROUP)),
-            pltpu.SemaphoreType.DMA((GROUP,)),
-            pltpu.SemaphoreType.DMA((GROUP,)),
+            pltpu.SemaphoreType.DMA((2,)),
+            pltpu.SemaphoreType.DMA((2,)),
+            pltpu.SemaphoreType.DMA((2,)),
+            pltpu.SemaphoreType.DMA((2,)),
+            pltpu.SemaphoreType.DMA,
+            pltpu.SemaphoreType.DMA,
             pltpu.SemaphoreType.DMA((5,)),
             pltpu.SemaphoreType.REGULAR((3,)),
         ],
@@ -481,7 +518,19 @@
             )
         )
     )
-    return decode(coded, CODE_SCALE), residual
+    return pl.pallas_call(
+        write_out,
+        out_shape=(
+            jax.ShapeDtypeStruct((ATOMS, SLAB), F32),
+            jax.ShapeDtypeStruct((CHANS, SLAB), F32),
+        ),
+        in_specs=[vmem] * 2,
+        out_specs=[pl.BlockSpec(memory_space=pltpu.HBM)] * 2,
+        scratch_shapes=[pltpu.VMEM((ATOMS, SLAB), F32), pltpu.SemaphoreType.DMA((5,))],
+    )(
+        pltpu.with_memory_space_constraint(coded, pltpu.VMEM),
+        pltpu.with_memory_space_constraint(residual, pltpu.VMEM),
+    )
 
 
 def solution(mesh):

time: 46 us -> 43.2 us (0.939)
  Pallas kernels: 43.5 us -> 41.9 us
  other arithmetic: 0.88 us -> 0 us
  local copies, waits for them, and re-layouts: 0.63 us -> 0 us
    pallas_call x1, Pallas kernels: 43.5 us -> 41.1 us  [body(): pl.pallas_call(functools.partial(kernel, lax.axis_size('tm')), out_shape=...]
    select_n x1 -> x0, other arithmetic: 0.88 us -> none  [decode(): return jnp.where(power < 0.0, -root, root)]
    pallas_call x0 -> x1, Pallas kernels: none -> 0.85 us  [body(): pl.pallas_call(write_out, out_shape=(jax.ShapeDtypeStruct((ATOMS, SLAB),...]
    unnamed x1 -> x0, local copies, waits for them, and re-layouts: 0.63 us -> none
where the time goes in v4:
time: 43.2 us; the launch traced here: 42.6 us
  Pallas kernels  41.9 us (97%)
  between operations  0.64 us (1%)
    pallas_call x1, Pallas kernels, body(): pl.pallas_call(functools.partial(kernel, lax.axis_size('tm')), out_shape=...  41.1 us

profile of v4, /device:TPU:1, one launch (start us, length us, event | category | flops | bytes accessed | tf_op | source)
XLA Modules:
  0.0 42.6 jit_solution(11042756935638977269)
XLA Ops:
  0.6 41.1 %shard_map.68 = (bf16[64,1024]{1,0:T(8,128)(2,1)S(1)}, f32[16,1024]{1,0:T(8,128)S(1)}) custom-call(bf16[1024,512]{1,0:T(8,128)(2,1)} %bitcast.3, f32[64,1024]{1,0:T(8,128)} %codes_hbm.1, bf16[16,1024]{1,0:T(8,128)(2,1)} %signal_hbm.1, f32[1,64]{1,0:T(1,128)} %bitcast.4, f32[1,64]{1,0:T(1,128)} %bitcast.5), custom_call_target="tpu_custom_call" | custom-call | tf_op jit(solution)/shard_map/pallas_call | solution.py:464
  41.7 0.9 %shard_map.69 = (f32[64,1024]{1,0:T(8,128)}, f32[16,1024]{1,0:T(8,128)}) custom-call(bf16[64,1024]{1,0:T(8,128)(2,1)S(1)} %get-tuple-element.4.coded, f32[16,1024]{1,0:T(8,128)S(1)} %get-tuple-element.5.residual), custom_call_target="tpu_custom_call" | custom-call | tf_op jit(solution)/shard_map/pallas_call | solution.py:521

commit v5 on v4

--- a/solution.py
+++ b/solution.py
@@ -44,7 +44,11 @@
             preferred_element_type=F32,
         ).astype(BF16)
         for j in range(8):
-            synthesis[16 * c : 16 * c + 16, 256 * j : 256 * j + 256] = turned[16 * j : 16 * j + 16, :]
+            for pair in range(2):
+                at = 1024 * pair + 128 * j
+                synthesis[16 * c : 16 * c + 16, at : at + 128] = turned[
+                    16 * j : 16 * j + 16, 128 * pair : 128 * pair + 128
+                ]
     row, column = tile_iota(512, 512, 0), tile_iota(512, 512, 1)
     select = (
         (row // 128 == column // 32 % 4)
@@ -55,7 +59,7 @@
         moved = matmul(natural[:, 512 * cg : 512 * cg + 512], select).astype(BF16)
         for h in range(4):
             for q in range(4):
-                at = 128 * (4 * cg + h)
+                at = 1024 * (h // 2) + 128 * (2 * cg + h % 2)
                 gradient[64 * q : 64 * q + 64, at : at + 128] = moved[
                     64 * h : 64 * h + 64, 128 * q : 128 * q + 128
                 ]
@@ -67,17 +71,21 @@
         shifted[j, :, place : place + keep] = pltpu.roll(codes, width - (113 - 16 * j), 1)[:, :keep]
 
 
-def synthesize(shifted, synthesis, spread, begin, end):
-    for start in range(begin, end, 256):
-        stop = min(start + 256, end)
-        total = None
-        for j in range(8):
-            window = jnp.concatenate(
-                [shifted[j, :, start - 128 * h + 384 : stop - 128 * h + 384] for h in range(4)], axis=0
-            )
-            part = matmul(synthesis[:, 256 * j : 256 * j + 256], window)
-            total = part if total is None else total + part
-        spread[:, start:stop] = total
+def multiply(weights, window_of, spread, begin, end, pairs, add):
+    window = jnp.concatenate([piece for pair in pairs for piece in window_of(pair)], axis=0)
+    total = matmul(weights[:, 1024 * pairs[0] : 1024 * pairs[-1] + 1024], window)
+    spread[:, begin:end] = spread[:, begin:end] + total if add else total
+
+
+def synthesize(shifted, synthesis, spread, begin, end, pairs=(0, 1), add=False):
+    def window_of(pair):
+        return [
+            shifted[j, :, begin - 128 * h + 384 : end - 128 * h + 384]
+            for j in range(8)
+            for h in (2 * pair, 2 * pair + 1)
+        ]
+
+    multiply(synthesis, window_of, spread, begin, end, pairs, add)
 
 
 def gather_rows(spread, begin):
@@ -103,23 +111,15 @@
         shifted[c // 4, at + 16 : at + 32, begin:end] = far[:, 128 * drop :]
 
 
-def correlate(shifted, gradient, spread, begin, end):
-    for start in range(begin, end, 256):
-        stop = min(start + 256, end)
-        total = None
-        for cg in range(4):
-            for h in (0, 2):
-                window = jnp.concatenate(
-                    [
-                        shifted[cg, :, start + 128 * h : stop + 128 * h],
-                        shifted[cg, :, start + 128 * h + 128 : stop + 128 * h + 128],
-                    ],
-                    axis=0,
-                )
-                at = 128 * (4 * cg + h)
-                part = matmul(gradient[:, at : at + 256], window)
-                total = part if total is None else total + part
-        spread[:, start:stop] = total
+def correlate(shifted, gradient, spread, begin, end, pairs=(0, 1), add=False):
+    def window_of(pair):
+        return [
+            shifted[cg, :, begin + 128 * h : end + 128 * h]
+            for cg in range(4)
+            for h in (2 * pair, 2 * pair + 1)
+        ]
+
+    multiply(gradient, window_of, spread, begin, end, pairs, add)
 
 
 def gather_taps(spread, begin):
@@ -157,7 +157,7 @@
     out_residual,
     bank,
     codes,
-    signal,
+    signal_in,
     step_size,
     threshold,
     natural,
@@ -168,23 +168,23 @@
     code_shift,
     spread,
     part,
+    coded_part,
     from_atom,
+    atom_tail,
     from_next,
+    from_before,
     misfit,
     misfit_shift,
     grad_send,
     grad_recv,
     code_send,
     scales,
-    halo_sems,
     part_send,
     part_recv,
     grad_send_sem,
     grad_recv_sem,
     code_send_sem,
     code_recv_sem,
-    edge_send_sem,
-    edge_recv_sem,
     load_sems,
     word,
 ):
@@ -192,7 +192,7 @@
     after, before = lax.rem(tm + 1, slabs), lax.rem(tm + slabs - 1, slabs)
     other = 1 - atom
     has_before, has_after = tm > 0, tm < slabs - 1
-    near_count = 6 + has_before.astype(jnp.int32) + has_after.astype(jnp.int32)
+    ends = has_before.astype(jnp.int32) + has_after.astype(jnp.int32)
     my_rows = pl.multiple_of(me // 4 * 16, 16)
     my_block = lax.rem(me, 4)
 
@@ -207,33 +207,29 @@
 
     barrier = pltpu.get_barrier_semaphore()
 
-    def near(signal_one):
-        @pl.when(has_after)
-        def _():
-            signal_one({"tm": after})
-
-        @pl.when(has_before)
-        def _():
-            signal_one({"tm": before})
-
-        for device in (
-            {"atom": other},
-            {"chan": me + 1 - 2 * lax.rem(me, 2)},
-            {"chan": me + 2 - 4 * lax.rem(me // 2, 2)},
-            {"chan": lax.rem(me + 4, GROUP)},
-            {"chan": lax.rem(me + 8, GROUP)},
-            {"chan": lax.rem(me + 12, GROUP)},
-        ):
-            signal_one(device)
-
-    near(lambda device: pl.semaphore_signal(barrier, 1, device_id=device, device_id_type=MESH))
+    def signal(semaphore, device):
+        pl.semaphore_signal(semaphore, 1, device_id=device, device_id_type=MESH)
+
+    def signal_group(semaphore):
+        for step in ((0, 0, 1), (0, 1, 0), (1, 0, 0), (2, 0, 0), (3, 0, 0)):
+            signal(semaphore, {"chan": at_step(step)})
+
+    for present, slab in ((has_after, after), (has_before, before)):
+
+        @pl.when(present)
+        def _(slab=slab):
+            signal(barrier, {"tm": slab, "atom": other})
+            signal(barrier, {"tm": slab})
+
+    signal_group(barrier)
+    signal(barrier, {"atom": other})
     loads = [
         pltpu.make_async_copy(source, target, load_sems.at[index])
         for index, (source, target) in enumerate(
             (
                 (codes_hbm, codes),
                 (bank_hbm, bank),
-                (signal_hbm, signal),
+                (signal_hbm, signal_in),
                 (step_size_hbm, step_size),
                 (threshold_hbm, threshold),
             )
@@ -242,25 +238,9 @@
     for load in loads:
         load.start()
 
-    def spread_word(stage):
-        near(
-            lambda device: pl.semaphore_signal(
-                word.at[stage], 1, device_id=device, device_id_type=MESH
-            )
-        )
-
-    halo = pltpu.make_async_remote_copy(
-        src_ref=lowered.at[2],
-        dst_ref=lowered.at[0],
-        send_sem=halo_sems.at[0],
-        recv_sem=halo_sems.at[1],
-        device_id={"tm": after},
-        device_id_type=MESH,
-    )
-
     @pl.when(jnp.logical_not(has_before))
     def _():
-        lowered[0] = jnp.zeros_like(lowered[0])
+        from_before[...] = jnp.zeros_like(from_before)
 
     @pl.when(jnp.logical_not(has_after))
     def _():
@@ -268,12 +248,9 @@
 
     loads[0].wait()
     for block in range(8):
-        lowered[1 + block // 4, block % 4] = codes[:, 128 * block : 128 * block + 128].astype(BF16)
+        lowered[block // 4, block % 4] = codes[:, 128 * block : 128 * block + 128].astype(BF16)
     for load in loads[1:]:
         load.wait()
-    pl.semaphore_wait(barrier, near_count)
-    spread_word(0)
-    pl.when(has_after)(halo.start)
     arrange_bank(bank, natural, synthesis, gradient)
     scales[:, 0:1] = column_of(step_size[...])
     scales[:, 1:2] = column_of(threshold[...])
@@ -281,24 +258,47 @@
         at = pl.multiple_of((my_block + 4 * half) * 128, 128)
         own[half] = codes[pl.ds(my_rows, 16), pl.ds(at, 128)]
 
+    code_shift[:, :, 256:384] = jnp.zeros((8, ATOMS, LANES), BF16)
+    code_shift[:, :, 1536:] = jnp.zeros((8, ATOMS, LANES), BF16)
+    spread[:, 1536:] = jnp.zeros((256, LANES), F32)
+    pl.semaphore_wait(barrier, 6 + 2 * ends)
+    signal_group(word.at[0])
+
+    nothing = jnp.zeros((ATOMS, LANES), BF16)
+
     def codes_of(first, last):
-        return jnp.concatenate([lowered[b // 4, b % 4] for b in range(first, last)], axis=1)
+        return [lowered[b // 4, b % 4] for b in range(first, last)]
+
+    def keep_part(sweep, which, recon):
+        if which < 2:
+            own_signal = signal_in[:, HALF * which : HALF * which + HALF].astype(F32)
+            recon = recon - jnp.where(atom == 0, own_signal, 0.0)
+        if which < 2:
+            part[sweep, which] = recon
+        if which != 1:
+            coded_part[sweep, which // 2] = encode(recon, GRAD_SCALE)
+
+    def early_half(sweep):
+        shift_codes(jnp.concatenate([nothing, *codes_of(0, 4), nothing], axis=1), 640, code_shift, 384)
+        synthesize(code_shift, synthesis, spread, 0, 256, (0,))
+        synthesize(code_shift, synthesis, spread, 256, 512)
+        synthesize(code_shift, synthesis, spread, 512, 640)
+        keep_part(sweep, 0, gather_rows(spread, 0))
+
+    def tail(sweep):
+        shift_codes(jnp.concatenate([*codes_of(3, 8), nothing], axis=1), 640, code_shift, 896)
+        synthesize(code_shift, synthesis, spread, 1024, 1280)
+        synthesize(code_shift, synthesis, spread, 1280, 1536, (1,))
+        keep_part(sweep, 2, gather_rows(spread, 1024))
 
     def late_half(sweep):
-        shift_codes(codes_of(4, 12), 1024, code_shift, 512)
-        synthesize(code_shift, synthesis, spread, 512, 1152)
-        recon = gather_rows(spread, 512)
-        part[sweep, 1] = recon - jnp.where(atom == 0, signal[:, HALF:].astype(F32), 0.0)
-
-    def early_half(sweep):
-        shift_codes(codes_of(0, 5), 512, code_shift, 0)
-        synthesize(code_shift, synthesis, spread, 0, 512)
-        recon = gather_rows(spread, 0)
-        part[sweep, 0] = recon - jnp.where(atom == 0, signal[:, :HALF].astype(F32), 0.0)
-
-    def part_copy(sweep, index, half, target, device):
+        synthesize(code_shift, synthesis, spread, 512, 768)
+        synthesize(code_shift, synthesis, spread, 768, 1024)
+        keep_part(sweep, 1, gather_rows(spread, 512))
+
+    def part_copy(sweep, index, source, target, device):
         return pltpu.make_async_remote_copy(
-            src_ref=part.at[sweep, half],
+            src_ref=source,
             dst_ref=target,
             send_sem=part_send.at[sweep, index],
             recv_sem=part_recv.at[sweep, index],
@@ -321,7 +321,7 @@
         if last:
             at = pl.multiple_of((my_block + 4 * half) * 128, 128)
             return out_codes.at[pl.ds(my_rows, 16), pl.ds(at, 128)]
-        return lowered.at[1 + half, my_block, pl.ds(my_rows, 16)]
+        return lowered.at[half, my_block, pl.ds(my_rows, 16)]
 
     def code_copy(last, half, step):
         return pltpu.make_async_remote_copy(
@@ -333,63 +333,82 @@
             device_id_type=MESH,
         )
 
-    def edge_copy(step):
-        return pltpu.make_async_remote_copy(
-            src_ref=code_send.at[1],
-            dst_ref=lowered.at[0, my_block, pl.ds(my_rows, 16)],
-            send_sem=edge_send_sem,
-            recv_sem=edge_recv_sem,
-            device_id={"tm": after, "chan": at_step(step)},
-            device_id_type=MESH,
-        )
-
     others = [step for step in STEPS if slot(step)]
 
     def wait_pieces(sem, first):
         pieces = grad_recv.at[0, first:]
         pltpu.make_async_copy(pieces, pieces, sem).wait()
-
-    def send_edges():
-        for step in STEPS:
-            edge_copy(step).start()
 
     sent = []
     for sweep in range(ITERS):
         last = sweep == ITERS - 1
         copies = [
-            part_copy(sweep, 0, 1, from_atom.at[sweep, 1], {"atom": other}),
-            part_copy(sweep, 1, 0, from_atom.at[sweep, 0], {"atom": other}),
-            part_copy(sweep, 2, 0, from_next.at[sweep, 0], {"tm": before}),
-            part_copy(sweep, 3, 0, from_next.at[sweep, 1], {"tm": before, "atom": other}),
+            part_copy(sweep, index, source, target, device)
+            for index, (source, target, device) in enumerate(
+                (
+                    (coded_part.at[sweep, 0], from_next.at[sweep, 1], {"tm": before, "atom": other}),
+                    (coded_part.at[sweep, 0], from_next.at[sweep, 0], {"tm": before}),
+                    (part.at[sweep, 0], from_atom.at[sweep, 0], {"atom": other}),
+                    (coded_part.at[sweep, 1], from_before.at[sweep, 1], {"tm": after, "atom": other}),
+                    (coded_part.at[sweep, 1], from_before.at[sweep, 0], {"tm": after}),
+                    (coded_part.at[sweep, 1], atom_tail.at[sweep], {"atom": other}),
+                    (part.at[sweep, 1], from_atom.at[sweep, 1], {"atom": other}),
+                )
+            )
         ]
+
+        def start(first, end):
+            for index in range(first, end):
+                if index < 2:
+                    pl.when(has_before)(copies[index].start)
+                elif index in (3, 4):
+                    pl.when(has_after)(copies[index].start)
+                else:
+                    copies[index].start()
+
+        if sweep:
+            wait_pieces(code_recv_sem.at[0], 1)
+        early_half(sweep)
+        start(0, 3)
+        if sweep:
+            wait_pieces(code_recv_sem.at[1], 1)
+        tail(sweep)
+        start(3, 6)
         late_half(sweep)
-        copies[0].start()
-        sent.extend(copies)
+        start(6, 7)
+        sent.append(copies)
         if sweep == 0:
-            pl.when(has_before)(halo.wait_recv)
-            pl.when(has_after)(halo.wait_send)
-            pl.semaphore_wait(word.at[0], near_count)
-            spread_word(1)
-        else:
-            pl.when(has_before)(lambda: wait_pieces(edge_recv_sem, 0))
-        early_half(sweep)
-        pl.when(has_before)(copies[3].start)
-        pl.when(has_before)(copies[2].start)
-        copies[1].start()
-
-        copies[0].wait_recv()
+            pl.semaphore_wait(word.at[0], 5)
+            signal_group(word.at[1])
+
+        def both(one, two):
+            return decode(one[...], GRAD_SCALE) + decode(two[...], GRAD_SCALE)
+
+        pl.when(has_after)(copies[0].wait_recv)
+        pl.when(has_after)(copies[1].wait_recv)
+        copies[5].wait_recv()
+        edge = both(from_next.at[sweep, 0], from_next.at[sweep, 1]) + both(
+            coded_part.at[sweep, 1], atom_tail.at[sweep]
+        )
+        misfit[:, SLAB:] = jnp.where(has_after, edge, 0.0)
+        copies[2].wait_recv()
+        pl.when(has_before)(copies[3].wait_recv)
+        pl.when(has_before)(copies[4].wait_recv)
+        whole = (part[sweep, 0] + from_atom[sweep, 0]) + both(
+            from_before.at[sweep, 0], from_before.at[sweep, 1]
+        )
+        misfit[:, :HALF] = whole
+        if last:
+            out_residual[:, :HALF] = whole
+        copies[6].wait_recv()
         whole = part[sweep, 1] + from_atom[sweep, 1]
         misfit[:, HALF:SLAB] = whole
         if last:
             out_residual[:, HALF:SLAB] = whole
-        shift_misfit(misfit, 4, 8, 1, misfit_shift)
-        copies[1].wait_recv()
-        whole = part[sweep, 0] + from_atom[sweep, 0]
-        misfit[:, :HALF] = whole
-        if last:
-            out_residual[:, :HALF] = whole
-        shift_misfit(misfit, 0, 5, 0, misfit_shift)
-        correlate(misfit_shift, gradient, spread, 0, 640)
+        shift_misfit(misfit, 0, 8, 0, misfit_shift)
+        correlate(misfit_shift, gradient, spread, 0, 128)
+        correlate(misfit_shift, gradient, spread, 128, 384)
+        correlate(misfit_shift, gradient, spread, 384, 640)
 
         def put(half):
             total = gather_taps(spread, HALF * half)
@@ -400,17 +419,14 @@
                 piece = total[row : row + 16, block : block + 128]
                 grad_send[half, owner] = encode(piece, GRAD_SCALE)
             if sweep == 0 and half == 0:
-                pl.semaphore_wait(word.at[1], near_count)
-                spread_word(2)
+                pl.semaphore_wait(word.at[1], 5)
             for step in others:
                 grad_copy(half, step).start()
 
         put(0)
-        pl.when(has_after)(copies[2].wait_recv)
-        pl.when(has_after)(copies[3].wait_recv)
-        misfit[:, SLAB:] = from_next[sweep, 0] + from_next[sweep, 1]
         shift_misfit(misfit, 7, 12, 1, misfit_shift)
-        correlate(misfit_shift, gradient, spread, 640, 1152)
+        correlate(misfit_shift, gradient, spread, 640, 896)
+        correlate(misfit_shift, gradient, spread, 896, 1152)
         put(1)
 
         for half in range(2):
@@ -425,26 +441,22 @@
             own[half] = updated
             if last:
                 wait_pieces(code_send_sem.at[half], 1)
-                if half == 1:
-                    pl.when(has_after)(lambda: wait_pieces(edge_send_sem, 0))
             code_send[half] = encode(updated, CODE_SCALE) if last else updated.astype(BF16)
             for step in others:
                 code_copy(last, half, step).start()
-            if half == 1 and not last:
-                pl.semaphore_wait(word.at[2], near_count)
-                pl.when(has_after)(send_edges)
             code_place(last, half)[...] = code_send[half]
-        for half in range(2):
-            wait_pieces(code_recv_sem.at[half], 1)
         if last:
             for half in range(2):
+                wait_pieces(code_recv_sem.at[half], 1)
                 wait_pieces(code_send_sem.at[half], 1)
                 wait_pieces(grad_send_sem.at[half], 1)
-            for index, copy in enumerate(sent):
-                if index % 4 < 2:
-                    copy.wait_send()
-                else:
-                    pl.when(has_before)(copy.wait_send)
+            for copy in (copy for group in sent for copy in group[:2]):
+                pl.when(has_before)(copy.wait_send)
+            for copy in (copy for group in sent for copy in group[3:5]):
+                pl.when(has_after)(copy.wait_send)
+            for group in sent:
+                for index in (2, 5, 6):
+                    group[index].wait_send()
 
 
 def write_out(coded, residual, out_codes, out_residual, plain, sems):
@@ -478,30 +490,30 @@
             pltpu.VMEM((256, 2048), BF16),
             pltpu.VMEM((256, 2048), BF16),
             pltpu.VMEM((256, 2048), BF16),
-            pltpu.VMEM((3, 4, ATOMS, LANES), BF16),
+            pltpu.VMEM((2, 4, ATOMS, LANES), BF16),
             pltpu.VMEM((2, 16, LANES), F32),
-            pltpu.VMEM((8, ATOMS, 1536), BF16),
-            pltpu.VMEM((256, 1152), F32),
+            pltpu.VMEM((8, ATOMS, 1664), BF16),
+            pltpu.VMEM((256, 1664), F32),
             pltpu.VMEM((ITERS, 2, CHANS, HALF), F32),
+            pltpu.VMEM((ITERS, 2, CHANS, HALF), BF16),
             pltpu.VMEM((ITERS, 2, CHANS, HALF), F32),
-            pltpu.VMEM((ITERS, 2, CHANS, HALF), F32),
+            pltpu.VMEM((ITERS, CHANS, HALF), BF16),
+            pltpu.VMEM((ITERS, 2, CHANS, HALF), BF16),
+            pltpu.VMEM((ITERS, 2, CHANS, HALF), BF16),
             pltpu.VMEM((CHANS, 1536), F32),
             pltpu.VMEM((4, 128, 1536), BF16),
             pltpu.VMEM((2, GROUP, 16, LANES), BF16),
             pltpu.VMEM((2, GROUP, 16, LANES), BF16),
             pltpu.VMEM((2, 16, LANES), BF16),
             pltpu.VMEM((ATOMS, LANES), F32),
-            pltpu.SemaphoreType.DMA((2,)),
-            pltpu.SemaphoreType.DMA((ITERS, 4)),
-            pltpu.SemaphoreType.DMA((ITERS, 4)),
+            pltpu.SemaphoreType.DMA((ITERS, 7)),
+            pltpu.SemaphoreType.DMA((ITERS, 7)),
             pltpu.SemaphoreType.DMA((2,)),
             pltpu.SemaphoreType.DMA((2,)),
             pltpu.SemaphoreType.DMA((2,)),
             pltpu.SemaphoreType.DMA((2,)),
-            pltpu.SemaphoreType.DMA,
-            pltpu.SemaphoreType.DMA,
             pltpu.SemaphoreType.DMA((5,)),
-            pltpu.SemaphoreType.REGULAR((3,)),
+            pltpu.SemaphoreType.REGULAR((2,)),
         ],
         compiler_params=pltpu.CompilerParams(
             collective_id=0, has_side_effects=True, vmem_limit_bytes=48 * 1024 * 1024

time: 43.2 us -> 42.4 us (0.981); the launches traced: 42.6 us -> 42.3 us
  no operation moved by 1% of the time
where the time goes in v5:
time: 42.4 us; the launch traced here: 42.3 us
  Pallas kernels  41.7 us (98%)
  between operations  0.64 us (2%)
    pallas_call x1, Pallas kernels, body(): pl.pallas_call(functools.partial(kernel, lax.axis_size('tm')), out_shape=...  40.8 us
    pallas_call x1, Pallas kernels, body(): pl.pallas_call(write_out, out_shape=(jax.ShapeDtypeStruct((ATOMS, SLAB),...  0.85 us

profile of v5, /device:TPU:1, one launch (start us, length us, event | category | flops | bytes accessed | tf_op | source)
XLA Modules:
  0.0 42.3 jit_solution(5778304534919969141)
XLA Ops:
  0.6 40.8 %shard_map.68 = (bf16[64,1024]{1,0:T(8,128)(2,1)S(1)}, f32[16,1024]{1,0:T(8,128)S(1)}) custom-call(bf16[1024,512]{1,0:T(8,128)(2,1)} %bitcast.3, f32[64,1024]{1,0:T(8,128)} %codes_hbm.1, bf16[16,1024]{1,0:T(8,128)(2,1)} %signal_hbm.1, f32[1,64]{1,0:T(1,128)} %bitcast.4, f32[1,64]{1,0:T(1,128)} %bitcast.5), custom_call_target="tpu_custom_call" | custom-call | tf_op jit(solution)/shard_map/pallas_call | solution.py:476
  41.4 0.9 %shard_map.69 = (f32[64,1024]{1,0:T(8,128)}, f32[16,1024]{1,0:T(8,128)}) custom-call(bf16[64,1024]{1,0:T(8,128)(2,1)S(1)} %get-tuple-element.4.coded, f32[16,1024]{1,0:T(8,128)S(1)} %get-tuple-element.5.residual), custom_call_target="tpu_custom_call" | custom-call | tf_op jit(solution)/shard_map/pallas_call | solution.py:533

commit v6 on v5

--- a/solution.py
+++ b/solution.py
@@ -400,13 +400,14 @@
         misfit[:, :HALF] = whole
         if last:
             out_residual[:, :HALF] = whole
+        shift_misfit(misfit, 0, 4, 0, misfit_shift)
+        correlate(misfit_shift, gradient, spread, 0, 128)
         copies[6].wait_recv()
         whole = part[sweep, 1] + from_atom[sweep, 1]
         misfit[:, HALF:SLAB] = whole
         if last:
             out_residual[:, HALF:SLAB] = whole
-        shift_misfit(misfit, 0, 8, 0, misfit_shift)
-        correlate(misfit_shift, gradient, spread, 0, 128)
+        shift_misfit(misfit, 3, 8, 1, misfit_shift)
         correlate(misfit_shift, gradient, spread, 128, 384)
         correlate(misfit_shift, gradient, spread, 384, 640)
 

time: 42.4 us -> 42.1 us (level)
  Pallas kernels: 41.7 us -> 41 us
    pallas_call x1, Pallas kernels: 40.8 us -> 40.1 us  [body(): pl.pallas_call(functools.partial(kernel, lax.axis_size('tm')), out_shape=...]
where the time goes in v6:
time: 42.1 us; the launch traced here: 41.6 us
  Pallas kernels  41 us (97%)
  between operations  0.64 us (2%)
    pallas_call x1, Pallas kernels, body(): pl.pallas_call(functools.partial(kernel, lax.axis_size('tm')), out_shape=...  40.1 us
    pallas_call x1, Pallas kernels, body(): pl.pallas_call(write_out, out_shape=(jax.ShapeDtypeStruct((ATOMS, SLAB),...  0.85 us

profile of v6, /device:TPU:1, one launch (start us, length us, event | category | flops | bytes accessed | tf_op | source)
XLA Modules:
  0.0 41.6 jit_solution(10963122955582113957)
XLA Ops:
  0.6 40.1 %shard_map.68 = (bf16[64,1024]{1,0:T(8,128)(2,1)S(1)}, f32[16,1024]{1,0:T(8,128)S(1)}) custom-call(bf16[1024,512]{1,0:T(8,128)(2,1)} %bitcast.3, f32[64,1024]{1,0:T(8,128)} %codes_hbm.1, bf16[16,1024]{1,0:T(8,128)(2,1)} %signal_hbm.1, f32[1,64]{1,0:T(1,128)} %bitcast.4, f32[1,64]{1,0:T(1,128)} %bitcast.5), custom_call_target="tpu_custom_call" | custom-call | tf_op jit(solution)/shard_map/pallas_call | solution.py:477
  40.8 0.9 %shard_map.69 = (f32[64,1024]{1,0:T(8,128)}, f32[16,1024]{1,0:T(8,128)}) custom-call(bf16[64,1024]{1,0:T(8,128)(2,1)S(1)} %get-tuple-element.4.coded, f32[16,1024]{1,0:T(8,128)S(1)} %get-tuple-element.5.residual), custom_call_target="tpu_custom_call" | custom-call | tf_op jit(solution)/shard_map/pallas_call | solution.py:534
